TPU v7x, 512 devices: a whole 4x8x8 slice. The times are simulated.
512 devices in a mesh: grp: 32 (over x, z), vocab: 16 (over y, core).
Axes of the slice: x: 4, y: 8, z: 8, core: 2. Of those that a mesh axis runs over, the one named last changes fastest.
Arguments:
- teacher_rows: bfloat16 [64, 8, 4096], P('grp', None, 'vocab'), may hold values from -160 to 160
- student_rows: bfloat16 [32, 8, 5120], P('grp', None, 'vocab'), may hold values from -160 to 160
- teacher_head: bfloat16 [4096, 131072], P(None, ('grp', 'vocab')), may hold values from -0.25 to 0.25
- student_head: bfloat16 [5120, 131072], P(None, ('grp', 'vocab')), may hold values from -0.25 to 0.25
- lengths: int32 [64], replicated, may hold values from 1 to 7, as said below
- owner: int32 [64], replicated, may hold values from 0 to 31, as said below
Outputs:
- divergence: float32 [32, 8], P('grp')
- grad_student: bfloat16 [32, 8, 5120], P('grp', None, 'vocab')
Inputs may be any that keep to these rules, and one draw needn't show every extreme that they name: All 2 sequences of one teacher group share one owner, and each student group owns the sequences of exactly one teacher group. The lengths of the 2 sequences of one teacher group sum to at most 8, and to exactly 8 for some group.
All inputs are finite; a program needn't handle non-finite values.
Results may differ from a plain program's by a relative error of at most 0.018.
Values may be sent and summed in bfloat16 or wider, within the bound.
No kernel may reach another device: no remote copies, remote signals or barrier semaphores. Data moves between devices by JAX's collectives and lax.ppermute only.
A program may use at most 64 MiB of HBM per device.

v0:
```python
import jax
import jax.numpy as jnp
from jax import lax
from jax.sharding import Mesh
from jax.sharding import PartitionSpec as P

GRP = ("grp_0", "grp_1")
VOCAB = ("vocab_0", "vocab_1")
GRP_VOCAB = ("grp_0", "grp_1", "vocab_0", "vocab_1")


def in_order(pieces, dim):
    pieces = jnp.moveaxis(pieces, 0, dim)
    shape = pieces.shape
    return pieces.reshape(*shape[:dim], shape[dim] * shape[dim + 1], *shape[dim + 2 :])


def one_gather(arrays, axis, dims):
    flat = jnp.concatenate([a.reshape(-1) for a in arrays])
    lines, at, outs = (lax.all_gather(flat, axis), 0, [])
    for a, dim in zip(arrays, dims):
        pieces = lines[:, at : at + a.size].reshape(-1, *a.shape)
        outs.append(in_order(pieces, dim))
        at += a.size
    return tuple(outs)


def stacked_from(shard, axes, sequence):
    pieces = shard
    for k in sequence:
        pieces = lax.all_gather(pieces, axes[k])
    done = sequence[::-1]
    back = [done.index(k) for k in range(len(axes))]
    pieces = pieces.transpose(*back, *range(len(axes), pieces.ndim))
    return pieces.reshape(-1, *shard.shape)


def gathered_by_axis(shard, axes, sequence, dim):
    return in_order(stacked_from(shard, axes, sequence), dim)


def collected_together(shard, axis):
    leaves = jax.tree.leaves(shard)
    sequence = sorted(range(len(leaves)), key=lambda k: -leaves[k].size)
    width = (1, *leaves[sequence[0]].shape)[-1]
    lines = [
        jnp.pad(leaves[k].reshape(-1), (0, -leaves[k].size % width)).reshape(-1, width)
        for k in sequence
    ]
    both, at, found = (lax.all_gather(jnp.concatenate(lines), axis), 0, {})
    for k, line in zip(sequence, lines):
        section = both[:, at : at + len(line)].reshape(len(both), -1)
        found[k] = section[:, : leaves[k].size].reshape(-1, *leaves[k].shape)
        at += len(line)
    numbers = iter(range(len(leaves)))
    return jax.tree.map(lambda _: found[next(numbers)], shard)


def combined_by_axis(shard, axes, combine):
    for axis in axes:
        pieces = collected_together(shard, axis)
        shard = jax.tree.map(lambda part: part[0], pieces)
        for k in range(1, lax.axis_size(axis)):
            shard = combine(shard, jax.tree.map(lambda part: part[k], pieces))
    return shard


def in_blocks(shard, dim, count):
    shape = shard.shape
    pieces = shard.reshape(*shape[:dim], count, shape[dim] // count, *shape[dim + 1 :])
    return jnp.moveaxis(pieces, dim, 0)


def sum_at_owner(shard, axis, dim):
    count = lax.axis_size(axis)
    pieces = lax.all_to_all(in_blocks(shard, dim, count), axis, 0, 0, tiled=True)
    return jnp.sum(pieces.astype(jnp.float32), axis=0)


def routing_tables(lengths, owner, groups, seq_count, positions, pad_rows):
    slot_count = seq_count * positions
    group_ids = jnp.arange(groups, dtype=jnp.int32)
    length_table = lengths.reshape(groups, seq_count)
    owner_table = owner.reshape(groups, seq_count)[:, 0]
    teacher_of = jnp.sum(
        (owner_table[None, :] == group_ids[:, None]).astype(jnp.int32) * group_ids[None, :], axis=1
    )
    position_ids = jnp.arange(positions, dtype=jnp.int32)
    live_slots = (position_ids[None, None, :] < length_table[:, :, None]).reshape(
        groups, slot_count
    )
    ranked = jnp.cumsum(live_slots.astype(jnp.int32), axis=1) - 1
    target = jnp.where(live_slots, ranked, pad_rows)
    matches = target[:, None, :] == jnp.arange(pad_rows, dtype=jnp.int32)[None, :, None]
    source = jnp.sum(
        matches.astype(jnp.int32) * jnp.arange(slot_count, dtype=jnp.int32)[None, None, :], axis=2
    )
    totals = jnp.sum(length_table, axis=1)
    owned_total = jnp.take(totals, teacher_of, axis=0)
    student_live = jnp.arange(pad_rows, dtype=jnp.int32)[None, :] < owned_total[:, None]
    return (teacher_of, source, student_live)


def combine(left_part, right_part):
    teacher_top = jnp.maximum(left_part[0], right_part[0])
    teacher_total = left_part[1] * jnp.exp(left_part[0] - teacher_top) + right_part[1] * jnp.exp(
        right_part[0] - teacher_top
    )
    student_top = jnp.maximum(left_part[2], right_part[2])
    left_scale = jnp.exp(left_part[2] - student_top)
    right_factor = jnp.exp(right_part[2] - student_top)
    student_total = left_part[3] * left_scale + right_part[3] * right_factor
    weighted = left_part[4] * left_scale + right_part[4] * right_factor
    return (teacher_top, teacher_total, student_top, student_total, weighted)


def per_device(teacher_rows, student_rows, teacher_head, student_head, lengths, owner):
    groups = lax.axis_size(GRP)
    seq_count = teacher_rows.shape[0]
    positions = teacher_rows.shape[1]
    slot_count = seq_count * positions
    pad_rows = student_rows.shape[1]
    own_group = lax.axis_index(GRP)
    teacher_of, source, student_live = routing_tables(
        lengths, owner, groups, seq_count, positions, pad_rows
    )
    local_teacher = teacher_rows.reshape(slot_count, teacher_rows.shape[2])
    local_student = student_rows.reshape(pad_rows, student_rows.shape[2])
    own_source = lax.dynamic_index_in_dim(source, own_group, 0, keepdims=False)
    sent_teacher = jnp.take(local_teacher, own_source, axis=0)
    row_position = teacher_of[:, None] * pad_rows + jnp.arange(pad_rows, dtype=jnp.int32)[None, :]
    teacher_full, student_full = one_gather((sent_teacher, local_student), VOCAB, (1, 1))
    raw_teacher = jnp.dot(
        lax.all_gather(teacher_full, GRP, axis=0, tiled=True),
        teacher_head,
        preferred_element_type=jnp.float32,
    )
    student_logits = jnp.dot(
        gathered_by_axis(student_full, GRP, (0, 1), 0),
        student_head,
        preferred_element_type=jnp.float32,
    )
    teacher_logits = jnp.take(raw_teacher, row_position.reshape(-1), axis=0)
    weight = student_live.reshape(-1).astype(jnp.float32)
    local_teacher_top = jnp.max(teacher_logits, axis=1)
    local_student_top = jnp.max(student_logits, axis=1)
    student_exp = jnp.exp(student_logits - local_student_top[:, None])
    merged = combined_by_axis(
        (
            local_teacher_top,
            jnp.sum(jnp.exp(teacher_logits - local_teacher_top[:, None]), axis=1),
            local_student_top,
            jnp.sum(student_exp, axis=1),
            jnp.sum(student_exp * (student_logits - teacher_logits), axis=1),
        ),
        GRP_VOCAB,
        combine,
    )
    teacher_lse = merged[0] + jnp.log(merged[1])
    student_lse = merged[2] + jnp.log(merged[3])
    log_q = student_logits - student_lse[:, None]
    log_p = teacher_logits - teacher_lse[:, None]
    student_prob = jnp.exp(log_q)
    log_ratio = log_q - log_p
    kl_rows = merged[4] / merged[3] - student_lse + teacher_lse
    kl_rows = kl_rows * weight
    grad_logits = (weight[:, None] * student_prob * (log_ratio - kl_rows[:, None])).astype(
        jnp.bfloat16
    )
    partial_value = jnp.einsum(
        "rv,dv->rd", grad_logits, student_head, preferred_element_type=jnp.float32
    )
    feature_totals_acc = sum_at_owner(partial_value.astype(jnp.bfloat16), VOCAB, 1)
    grad_rows = sum_at_owner(feature_totals_acc.astype(jnp.bfloat16), GRP, 0).astype(jnp.bfloat16)
    divergence = lax.dynamic_slice_in_dim(kl_rows, own_group * pad_rows, pad_rows, 0)
    return (divergence.reshape(1, pad_rows), grad_rows.reshape(1, pad_rows, grad_rows.shape[1]))


def solution(mesh):
    torus = Mesh(mesh.devices.reshape(4, 8, 8, 2), ("grp_0", "grp_1", "vocab_0", "vocab_1"))
    return jax.shard_map(
        per_device,
        mesh=torus,
        in_specs=(
            P(GRP, None, VOCAB),
            P(GRP, None, VOCAB),
            P(None, GRP_VOCAB),
            P(None, GRP_VOCAB),
            P(),
            P(),
        ),
        out_specs=(P(GRP, None), P(GRP, None, VOCAB)),
        check_vma=False,
    )
```

profile of v0, /device:TPU:1, one launch (start us, length us, event | category | flops | bytes accessed | tf_op | source)
XLA Modules:
  0.0 332.1 jit_solution(13637512223904512838)
XLA Ops:
  7.2 0.9 reshape.2804
  8.9 0.8 reshape_reshape.6
  9.7 1.3 gather_fusion.1
  11.1 21.7 %all-gather.6 = bf16[16,1,4608]{2,1,0:T(2,128)(2,1)S(1)} all-gather(bf16[1,1,4608]{2,1,0:T(2,128)(2,1)S(1)} %reshape.2848), channel_id=2, replica_groups=mesh['grp_0'=4,'grp_1'=8,'vocab_0'=8,'vocab_1'=2] {'vocab_0','vocab_1'}, dimensions={0}, use_global_device_ids=true | all-gather | bytes 156672 | tf_op jit(solution)/shard_map/all_gather | solution.py:20
  33.8 10.2 %all_gather.45 = bf16[4,8,5120]{2,1,0:T(8,128)(2,1)} all-gather(bf16[1,8,5120]{2,1,0:T(8,128)(2,1)S(1)} %all_gather_reshape.3), channel_id=1, replica_groups=mesh['grp_0'=4,'grp_1'=8,'vocab_0'=8,'vocab_1'=2] {'grp_0'}, dimensions={0}, use_global_device_ids=true | all-gather | bytes 409600 | tf_op jit(solution)/shard_map/all_gather | solution.py:31
  44.5 0.7 gather_fusion
  45.7 67.2 %all-gather.14.cloned.1.call-done = bf16[256,4096]{1,0:T(8,128)(2,1)} async-done(((bf16[8,4096]{1,0:T(8,128)(2,1)}), bf16[256,4096]{1,0:T(8,128)(2,1)}) %all-gather.14.cloned.1.call-update) | async-done | bytes 2097168 | tf_op jit(solution)/shard_map/all_gather | solution.py:134
  113.0 2.9 fusion.212
  115.9 1.0 gather_fusion.2
  117.1 41.4 %all-gather.16.cloned.1.call-done = bf16[32,8,5120]{2,1,0:T(8,128)(2,1)} async-done(((bf16[4,8,5120]{2,1,0:T(8,128)(2,1)}), bf16[32,8,5120]{2,1,0:T(8,128)(2,1)}) %all-gather.16.cloned.1.call-update) | async-done | bytes 2621456 | tf_op jit(solution)/shard_map/all_gather | solution.py:31
  158.4 1.9 copy.40
  160.4 1.1 fusion.211
  161.7 9.3 %all-gather.7 = f32[4,5,256]{2,1,0:T(8,128)S(1)} all-gather(f32[1,5,256]{2,1,0:T(8,128)S(1)} %bitcast.1105), channel_id=4, replica_groups=mesh['grp_0'=4,'grp_1'=8,'vocab_0'=8,'vocab_1'=2] {'grp_0'}, dimensions={0}, use_global_device_ids=true | all-gather | bytes 25600 | tf_op jit(solution)/shard_map/all_gather | solution.py:50
  171.1 18.3 %all-gather.8 = f32[8,5,256]{2,1,0:T(8,128)S(1)} all-gather(f32[1,5,256]{2,1,0:T(8,128)S(1)} %bitcast.1106), channel_id=5, replica_groups=mesh['grp_0'=4,'grp_1'=8,'vocab_0'=8,'vocab_1'=2] {'grp_1'}, dimensions={0}, use_global_device_ids=true | all-gather | bytes 46080 | tf_op jit(solution)/shard_map/all_gather | solution.py:50
  189.6 19.3 %all-gather.9 = f32[8,5,256]{2,1,0:T(8,128)S(1)} all-gather(f32[1,5,256]{2,1,0:T(8,128)S(1)} %bitcast.1107), channel_id=6, replica_groups=mesh['grp_0'=4,'grp_1'=8,'vocab_0'=8,'vocab_1'=2] {'vocab_0'}, dimensions={0}, use_global_device_ids=true | all-gather | bytes 46080 | tf_op jit(solution)/shard_map/all_gather | solution.py:50
  209.0 20.9 %all-gather.10 = f32[2,5,256]{2,1,0:T(8,128)S(1)} all-gather(f32[1,5,256]{2,1,0:T(8,128)S(1)} %bitcast.1108), channel_id=7, replica_groups=mesh['grp_0'=4,'grp_1'=8,'vocab_0'=8,'vocab_1'=2] {'vocab_1'}, dimensions={0}, use_global_device_ids=true | all-gather | bytes 15360 | tf_op jit(solution)/shard_map/all_gather | solution.py:50
  229.9 2.5 convolution_convert_fusion
  232.4 4.4 %copy.41 = bf16[256,5120]{0,1:T(8,128)(2,1)} copy(bf16[256,5120]{1,0:T(8,128)(2,1)} %convolution_convert_fusion) | data formatting | bytes 5242880 | tf_op jit(solution)/shard_map/convert_element_type | solution.py:173
  236.8 68.4 %all_to_all.10 = bf16[16,256,320]{1,2,0:T(8,128)(2,1)} all-to-all(bf16[16,256,320]{1,2,0:T(8,128)(2,1)} %bitcast.1097), channel_id=1, replica_groups=mesh['grp_0'=4,'grp_1'=8,'vocab_0'=8,'vocab_1'=2] {'vocab_0','vocab_1'}, dimensions={0} | all-to-all | bytes 5242880 | tf_op jit(solution)/shard_map/all_to_all | solution.py:76
  305.1 2.1 reduce_sum.87
  307.3 0.8 copy.42
  308.1 6.0 %all-to-all-start.1 = ((bf16[32,8,320]{2,1,0:T(8,128)(2,1)}), bf16[32,8,320]{2,1,0:T(8,128)(2,1)S(1)}, u32[]{:S(2)}, u32[]{:S(2)}) async-start(bf16[32,8,320]{2,1,0:T(8,128)(2,1)} %bitcast.134), calls=%async_computation.1 | async-start | bytes 393216 | tf_op jit(solution)/shard_map/all_to_all | solution.py:76
  314.7 10.0 %all-to-all-done.1 = bf16[32,8,320]{2,1,0:T(8,128)(2,1)S(1)} async-done(((bf16[32,8,320]{2,1,0:T(8,128)(2,1)}), bf16[32,8,320]{2,1,0:T(8,128)(2,1)S(1)}, u32[]{:S(2)}, u32[]{:S(2)}) %all-to-all-start.1) | async-done | bytes 163872 | tf_op jit(solution)/shard_map/all_to_all | solution.py:76
  324.6 0.6 reduce_sum.88
  (67 shorter events, 4.1 us)
Async XLA Ops:
  7.2 153.2 %copy-start = (bf16[5120,256]{1,0:T(8,128)(2,1)S(1)}, bf16[5120,256]{1,0:T(8,128)(2,1)}, u32[]{:S(2)}) copy-start(bf16[5120,256]{1,0:T(8,128)(2,1)} %param.9) | copy-start | bytes 7864324
  7.2 37.0 %copy-start.1 = (s32[64]{0:T(128)S(1)}, s32[64]{0:T(128)}, u32[]{:S(2)}) copy-start(s32[64]{0:T(128)} %param.11) | copy-start | bytes 772
  7.2 105.8 %all-gather.14.cloned.1.call-start = ((), (), s32[]{:S(2)}) async-start(), calls=%async_computation.2 | async-start | bytes 2162688 | tf_op jit(solution)/shard_map/all_gather | solution.py:134
  33.4 125.0 %all-gather.16.cloned.1.call-start = ((), (), s32[]{:S(2)}) async-start(), calls=%async_computation.3 | async-start | bytes 2949120 | tf_op jit(solution)/shard_map/all_gather | solution.py:31
  308.1 16.6 %all-to-all-start.1 = ((bf16[32,8,320]{2,1,0:T(8,128)(2,1)}), bf16[32,8,320]{2,1,0:T(8,128)(2,1)S(1)}, u32[]{:S(2)}, u32[]{:S(2)}) async-start(bf16[32,8,320]{2,1,0:T(8,128)(2,1)} %bitcast.134), calls=%async_computation.1 | async-start | bytes 393216 | tf_op jit(solution)/shard_map/all_to_all | solution.py:76
Sparse Core Ops, SparseCore 0:
  33.6 79.3 all-gather.13
  115.1 43.3 all-gather.15
where the time goes:
time: 333 us; the launch traced here: 332 us
  blocking collectives  168 us (50%)
  waiting for transfers between devices  119 us (36%)
  local copies, waits for them, and re-layouts  14.5 us (4%)
  between operations  14.3 us (4%)
  matrix products  6.54 us (2%)
  starting transfers between devices  6.08 us (2%)
  other arithmetic  3.99 us (1%)
    all_to_all x1, blocking collectives, sum_at_owner(): lax.all_to_all(in_blocks(shard, dim, count), axis, 0, 0, tiled=True)  68.4 us
    all_gather x4, blocking collectives, collected_together(): both, at, found = (lax.all_gather(jnp.concatenate(lines), axis), 0, {})  67.8 us
    all_gather x1, waiting for transfers between devices, per_device(): lax.all_gather(teacher_full, GRP, axis=0, tiled=True)  67.2 us
    all_gather x1, waiting for transfers between devices, stacked_from(): pieces = lax.all_gather(pieces, axes[k])  41.4 us
    all_gather x1, blocking collectives, one_gather(): lines, at, outs = (lax.all_gather(flat, axis), 0, [])  21.7 us
    all_gather x1, blocking collectives, stacked_from(): pieces = lax.all_gather(pieces, axes[k])  10.2 us
    all_to_all x1, waiting for transfers between devices, sum_at_owner(): lax.all_to_all(in_blocks(shard, dim, count), axis, 0, 0, tiled=True)  9.96 us
  transfers between devices with their start and end apart: 3, of which 3 were waited for; matrix products, arithmetic and copies ran while one was open for 2% of the time, Pallas kernels for 0%

commit v1 on v0

--- a/solution.py
+++ b/solution.py
@@ -3,10 +3,18 @@
 from jax import lax
 from jax.sharding import Mesh
 from jax.sharding import PartitionSpec as P
+from jax.lax import all_to_all, axis_size
 
 GRP = ("grp_0", "grp_1")
 VOCAB = ("vocab_0", "vocab_1")
 GRP_VOCAB = ("grp_0", "grp_1", "vocab_0", "vocab_1")
+
+
+def _watch_shelves(local_values):
+    piece_next = jnp.concatenate(
+        all_to_all(jnp.stack([local_values] * axis_size(GRP)), GRP, 0, 0), axis=0
+    )
+    return piece_next
 
 
 def in_order(pieces, dim):
@@ -131,9 +139,7 @@
     row_position = teacher_of[:, None] * pad_rows + jnp.arange(pad_rows, dtype=jnp.int32)[None, :]
     teacher_full, student_full = one_gather((sent_teacher, local_student), VOCAB, (1, 1))
     raw_teacher = jnp.dot(
-        lax.all_gather(teacher_full, GRP, axis=0, tiled=True),
-        teacher_head,
-        preferred_element_type=jnp.float32,
+        _watch_shelves(teacher_full), teacher_head, preferred_element_type=jnp.float32
     )
     student_logits = jnp.dot(
         gathered_by_axis(student_full, GRP, (0, 1), 0),

time: 333 us -> 300 us (0.901)
  waiting for transfers between devices: 119 us -> 78 us
  starting transfers between devices: 6.08 us -> 16.9 us
  blocking collectives: 168 us -> 164 us
    all_gather x1 -> x0, waiting for transfers between devices: 67.2 us -> none  [per_device(): lax.all_gather(teacher_full, GRP, axis=0, tiled=True)]
    all_to_all x0 -> x1, waiting for transfers between devices: none -> 59.1 us  [_watch_shelves(): all_to_all(jnp.stack([local_values] * axis_size(GRP)), GRP, 0, 0)]
    all_gather x1, waiting for transfers between devices: 41.4 us -> 8.83 us  [stacked_from(): pieces = lax.all_gather(pieces, axes[k])]
    all_to_all x0 -> x1, starting transfers between devices: none -> 10.9 us  [_watch_shelves(): all_to_all(jnp.stack([local_values] * axis_size(GRP)), GRP, 0, 0)]
  transfers between devices with their start and end apart: 3 -> 3, of which waited for: 3 -> 3; matrix products, arithmetic and copies ran while one was open for 2% -> 3% of each run, Pallas kernels for 0% -> 0%
where the time goes in v1:
time: 300 us; the launch traced here: 299 us
  blocking collectives  164 us (55%)
  waiting for transfers between devices  78 us (26%)
  starting transfers between devices  16.9 us (6%)
  local copies, waits for them, and re-layouts  15.5 us (5%)
  between operations  14.3 us (5%)
  matrix products  6.54 us (2%)
  other arithmetic  3.98 us (1%)
    all_to_all x1, blocking collectives, sum_at_owner(): lax.all_to_all(in_blocks(shard, dim, count), axis, 0, 0, tiled=True)  66.9 us
    all_gather x4, blocking collectives, collected_together(): both, at, found = (lax.all_gather(jnp.concatenate(lines), axis), 0, {})  65.3 us
    all_to_all x1, waiting for transfers between devices, _watch_shelves(): all_to_all(jnp.stack([local_values] * axis_size(GRP)), GRP, 0, 0)  59.1 us
    all_gather x1, blocking collectives, one_gather(): lines, at, outs = (lax.all_gather(flat, axis), 0, [])  21.7 us
    all_to_all x1, starting transfers between devices, _watch_shelves(): all_to_all(jnp.stack([local_values] * axis_size(GRP)), GRP, 0, 0)  10.9 us
    all_gather x1, blocking collectives, stacked_from(): pieces = lax.all_gather(pieces, axes[k])  10.2 us
    all_to_all x1, waiting for transfers between devices, sum_at_owner(): lax.all_to_all(in_blocks(shard, dim, count), axis, 0, 0, tiled=True)  9.97 us
    all_gather x1, waiting for transfers between devices, stacked_from(): pieces = lax.all_gather(pieces, axes[k])  8.83 us
  transfers between devices with their start and end apart: 3, of which 3 were waited for; matrix products, arithmetic and copies ran while one was open for 3% of the time, Pallas kernels for 0%

profile of v1, /device:TPU:1, one launch (start us, length us, event | category | flops | bytes accessed | tf_op | source)
XLA Modules:
  0.0 299.3 jit_solution(10105985711036775779)
XLA Ops:
  7.3 0.9 reshape.2806
  8.9 0.8 reshape_reshape.6
  9.7 1.3 gather_fusion.1
  11.1 21.7 %all-gather.6 = bf16[16,1,4608]{2,1,0:T(2,128)(2,1)S(1)} all-gather(bf16[1,1,4608]{2,1,0:T(2,128)(2,1)S(1)} %reshape.2850), channel_id=2, replica_groups=mesh['grp_0'=4,'grp_1'=8,'vocab_0'=8,'vocab_1'=2] {'vocab_0','vocab_1'}, dimensions={0}, use_global_device_ids=true | all-gather | bytes 156672 | tf_op jit(solution)/shard_map/all_gather | solution.py:28
  33.1 10.2 %all_gather.41 = bf16[4,8,5120]{2,1,0:T(8,128)(2,1)} all-gather(bf16[1,8,5120]{2,1,0:T(8,128)(2,1)S(1)} %all_gather_reshape.3), channel_id=1, replica_groups=mesh['grp_0'=4,'grp_1'=8,'vocab_0'=8,'vocab_1'=2] {'grp_0'}, dimensions={0}, use_global_device_ids=true | all-gather | bytes 409600 | tf_op jit(solution)/shard_map/all_gather | solution.py:39
  43.4 1.6 stack.3
  45.0 10.9 %all-to-all-start = ((bf16[32,8,4096]{2,1,0:T(8,128)(2,1)}), bf16[32,8,4096]{2,1,0:T(8,128)(2,1)}, u32[]{:S(2)}, u32[]{:S(2)}) async-start(bf16[32,8,4096]{2,1,0:T(8,128)(2,1)} %stack.3), calls=%async_computation | async-start | bytes 4194304 | tf_op jit(solution)/shard_map/all_to_all | solution.py:15
  57.6 59.1 %all-to-all-done = bf16[32,8,4096]{2,1,0:T(8,128)(2,1)} async-done(((bf16[32,8,4096]{2,1,0:T(8,128)(2,1)}), bf16[32,8,4096]{2,1,0:T(8,128)(2,1)}, u32[]{:S(2)}, u32[]{:S(2)}) %all-to-all-start) | async-done | bytes 2097184 | tf_op jit(solution)/shard_map/all_to_all | solution.py:15
  116.7 2.9 fusion
  119.7 1.0 gather_fusion.2
  120.8 8.8 %all-gather.13.cloned.1.call-done = bf16[32,8,5120]{2,1,0:T(8,128)(2,1)} async-done(((bf16[4,8,5120]{2,1,0:T(8,128)(2,1)}), bf16[32,8,5120]{2,1,0:T(8,128)(2,1)}) %all-gather.13.cloned.1.call-update) | async-done | bytes 2621456 | tf_op jit(solution)/shard_map/all_gather | solution.py:39
  129.7 1.9 copy.40
  131.6 1.1 fusion.213
  132.9 9.3 %all-gather.7 = f32[4,5,256]{2,1,0:T(8,128)S(1)} all-gather(f32[1,5,256]{2,1,0:T(8,128)S(1)} %bitcast.1107), channel_id=4, replica_groups=mesh['grp_0'=4,'grp_1'=8,'vocab_0'=8,'vocab_1'=2] {'grp_0'}, dimensions={0}, use_global_device_ids=true | all-gather | bytes 25600 | tf_op jit(solution)/shard_map/all_gather | solution.py:58
  142.3 18.2 %all-gather.8 = f32[8,5,256]{2,1,0:T(8,128)S(1)} all-gather(f32[1,5,256]{2,1,0:T(8,128)S(1)} %bitcast.1108), channel_id=5, replica_groups=mesh['grp_0'=4,'grp_1'=8,'vocab_0'=8,'vocab_1'=2] {'grp_1'}, dimensions={0}, use_global_device_ids=true | all-gather | bytes 46080 | tf_op jit(solution)/shard_map/all_gather | solution.py:58
  160.7 18.3 %all-gather.9 = f32[8,5,256]{2,1,0:T(8,128)S(1)} all-gather(f32[1,5,256]{2,1,0:T(8,128)S(1)} %bitcast.1109), channel_id=6, replica_groups=mesh['grp_0'=4,'grp_1'=8,'vocab_0'=8,'vocab_1'=2] {'vocab_0'}, dimensions={0}, use_global_device_ids=true | all-gather | bytes 46080 | tf_op jit(solution)/shard_map/all_gather | solution.py:58
  179.1 19.5 %all-gather.10 = f32[2,5,256]{2,1,0:T(8,128)S(1)} all-gather(f32[1,5,256]{2,1,0:T(8,128)S(1)} %bitcast.1110), channel_id=7, replica_groups=mesh['grp_0'=4,'grp_1'=8,'vocab_0'=8,'vocab_1'=2] {'vocab_1'}, dimensions={0}, use_global_device_ids=true | all-gather | bytes 15360 | tf_op jit(solution)/shard_map/all_gather | solution.py:58
  198.7 2.5 convolution_convert_fusion
  201.1 4.4 %copy.41 = bf16[256,5120]{0,1:T(8,128)(2,1)} copy(bf16[256,5120]{1,0:T(8,128)(2,1)} %convolution_convert_fusion) | data formatting | bytes 5242880 | tf_op jit(solution)/shard_map/convert_element_type | solution.py:179
  205.5 66.9 %all_to_all.15 = bf16[16,256,320]{1,2,0:T(8,128)(2,1)} all-to-all(bf16[16,256,320]{1,2,0:T(8,128)(2,1)} %bitcast.1099), channel_id=1, replica_groups=mesh['grp_0'=4,'grp_1'=8,'vocab_0'=8,'vocab_1'=2] {'vocab_0','vocab_1'}, dimensions={0} | all-to-all | bytes 5242880 | tf_op jit(solution)/shard_map/all_to_all | solution.py:84
  272.4 2.1 reduce_sum.87
  274.5 0.8 copy.42
  275.3 5.9 %all-to-all-start.2 = ((bf16[32,8,320]{2,1,0:T(8,128)(2,1)}), bf16[32,8,320]{2,1,0:T(8,128)(2,1)S(1)}, u32[]{:S(2)}, u32[]{:S(2)}) async-start(bf16[32,8,320]{2,1,0:T(8,128)(2,1)} %bitcast.135), calls=%async_computation.2 | async-start | bytes 393216 | tf_op jit(solution)/shard_map/all_to_all | solution.py:84
  281.8 10.0 %all-to-all-done.2 = bf16[32,8,320]{2,1,0:T(8,128)(2,1)S(1)} async-done(((bf16[32,8,320]{2,1,0:T(8,128)(2,1)}), bf16[32,8,320]{2,1,0:T(8,128)(2,1)S(1)}, u32[]{:S(2)}, u32[]{:S(2)}) %all-to-all-start.2) | async-done | bytes 163872 | tf_op jit(solution)/shard_map/all_to_all | solution.py:84
  (67 shorter events, 4.8 us)
Async XLA Ops:
  7.2 124.4 %copy-start = (bf16[5120,256]{1,0:T(8,128)(2,1)S(1)}, bf16[5120,256]{1,0:T(8,128)(2,1)}, u32[]{:S(2)}) copy-start(bf16[5120,256]{1,0:T(8,128)(2,1)} %param.9) | copy-start | bytes 7864324
  7.2 122.5 %all-gather.13.cloned.1.call-start = ((), (), s32[]{:S(2)}) async-start(), calls=%async_computation.3 | async-start | bytes 2949120 | tf_op jit(solution)/shard_map/all_gather | solution.py:39
  45.0 11.1 %copy-start.1 = (s32[64]{0:T(128)S(1)}, s32[64]{0:T(128)}, u32[]{:S(2)}) copy-start(s32[64]{0:T(128)} %param.11) | copy-start | bytes 772
  45.0 71.7 %all-to-all-start = ((bf16[32,8,4096]{2,1,0:T(8,128)(2,1)}), bf16[32,8,4096]{2,1,0:T(8,128)(2,1)}, u32[]{:S(2)}, u32[]{:S(2)}) async-start(bf16[32,8,4096]{2,1,0:T(8,128)(2,1)} %stack.3), calls=%async_computation | async-start | bytes 4194304 | tf_op jit(solution)/shard_map/all_to_all | solution.py:15
  275.3 16.5 %all-to-all-start.2 = ((bf16[32,8,320]{2,1,0:T(8,128)(2,1)}), bf16[32,8,320]{2,1,0:T(8,128)(2,1)S(1)}, u32[]{:S(2)}, u32[]{:S(2)}) async-start(bf16[32,8,320]{2,1,0:T(8,128)(2,1)} %bitcast.135), calls=%async_computation.2 | async-start | bytes 393216 | tf_op jit(solution)/shard_map/all_to_all | solution.py:84
Sparse Core Ops, SparseCore 0:
  43.5 86.1 all-gather.12
